TPU v7x, 32 devices: a whole 2x2x4 slice. The times are simulated.
32 devices in a mesh: rep: 1, dev: 32 (over z, y, x, core).
Axes of the slice: x: 2, y: 2, z: 4, core: 2. Of those that a mesh axis runs over, the one named last changes fastest.
Arguments:
- tokens: bfloat16 [4096, 7168], P(('rep', 'dev')), may hold values from -6 to 6
- routes: int32 [4096, 2], P(('rep', 'dev')), may hold values from 0 to 3, all different within a row; in each aligned block of 128 rows (0 to 127, 128 to 255, ...) at most 72 rows name the same one
- route_weight: bfloat16 [4096, 2], P(('rep', 'dev')), may hold values from 0.099609375 to 1
- gate_values: bfloat16 [28672, 1024], P('dev'), may hold values from -0.0625 to 0.0625
- gate_scales: float32 [224, 8], P('dev'), may hold values from 0.5 to 2
- up_values: bfloat16 [28672, 1024], P('dev'), may hold values from -0.0625 to 0.0625
- up_scales: float32 [224, 8], P('dev'), may hold values from 0.5 to 2
- down_values: bfloat16 [1024, 28672], P(None, 'dev'), may hold values from -0.1875 to 0.1875
- down_scales: float32 [8, 224], P(None, 'dev'), may hold values from 0.5 to 2
Outputs:
- mixed: bfloat16 [4096, 7168], P(('rep', 'dev'))
Inputs may be any that keep to these rules, and one draw needn't show every extreme that they name: `routes`: each token names 2 different experts. Among the tokens of one device (aligned blocks of 128 rows) no expert is named by more than 72 tokens, a bound that some block reaches.
All inputs are finite; a program needn't handle non-finite values.
Results may differ from a plain program's by a relative error of at most 0.0078.
Values may be sent and summed in bfloat16 or wider, within the bound.
A program may use at most 128 MiB of HBM per device.

v0:
```python
import jax
import jax.numpy as jnp
from jax import lax
from jax.sharding import PartitionSpec as P

BLOCK = 128
GROUP = 8


def from_partner(block, axis, stride):
    count = lax.axis_size(axis)
    route = []
    for low in range(count):
        high = low | 1 << stride
        if high != low and high < count:
            route += [(low, high), (high, low)]
    return lax.ppermute(block, axis, route)


def dequantize(values, scales):
    rows_count, cols_count = values.shape
    grid = values.astype(jnp.float32).reshape(
        rows_count // BLOCK, BLOCK, cols_count // BLOCK, BLOCK
    )
    return (grid * scales[:, None, :, None]).reshape(rows_count, cols_count).astype(jnp.bfloat16)


def slot_tables(routes, route_weight, experts, capacity):
    tok_count, top_count = routes.shape
    flat_routes = routes.reshape(-1)
    one_hot = (flat_routes[:, None] == jnp.arange(experts, dtype=jnp.int32)[None, :]).astype(
        jnp.int32
    )
    position = jnp.sum((jnp.cumsum(one_hot, axis=0) - 1) * one_hot, axis=1)
    slot_ids = (flat_routes * capacity + position).reshape(tok_count, top_count)
    slot_range = jnp.arange(experts * capacity, dtype=jnp.int32)
    placing = jnp.zeros((experts * capacity, tok_count), jnp.float32)
    weighting = jnp.zeros((experts * capacity, tok_count), jnp.float32)
    for choose in range(top_count):
        match = (slot_ids[:, choose][None, :] == slot_range[:, None]).astype(jnp.float32)
        placing = placing + match
        weighting = weighting + match * route_weight[:, choose].astype(jnp.float32)[None, :]
    shape_out = (experts, capacity, tok_count)
    return (
        placing.astype(jnp.bfloat16).reshape(shape_out),
        weighting.astype(jnp.bfloat16).reshape(shape_out),
    )


def upper_offset(bit_number, half_size):
    device_pos = lax.axis_index("dev")
    return (device_pos >> bit_number & 1) * half_size


def reduce_halves(stacked, split_dim, bit_list):
    for bit_number in bit_list:
        half_size = stacked.shape[split_dim] // 2
        keep_start = upper_offset(bit_number, half_size)
        kept_half = lax.dynamic_slice_in_dim(stacked, keep_start, half_size, axis=split_dim)
        sent_half = lax.dynamic_slice_in_dim(
            stacked, half_size - keep_start, half_size, axis=split_dim
        )
        stacked = kept_half + from_partner(sent_half, "dev", bit_number)
    return stacked


def ordered_pair(mine, theirs, keep_start, join_dim):
    doubled = jnp.concatenate([theirs, theirs], axis=join_dim)
    return lax.dynamic_update_slice_in_dim(doubled, mine, keep_start, axis=join_dim)


def join_halves(piece, join_dim, bit_list):
    for bit_number in bit_list[::-1]:
        partner = from_partner(piece, "dev", bit_number)
        keep_start = upper_offset(bit_number, piece.shape[join_dim])
        piece = ordered_pair(piece, partner, keep_start, join_dim)
    return piece


def shards(
    tokens,
    routes,
    route_weight,
    gate_values,
    gate_scales,
    up_values,
    up_scales,
    down_values,
    down_scales,
):
    devices = lax.axis_size("dev")
    experts = devices // GROUP
    tok_count = tokens.shape[0]
    top_count = routes.shape[1]
    capacity = min(tok_count, tok_count * top_count * 9 // (8 * experts))
    width_dev = gate_values.shape[0]
    placing, weighting = slot_tables(routes, route_weight, experts, capacity)
    split_tokens = tokens.reshape(tok_count, GROUP, width_dev)
    outgoing = jnp.einsum(
        "ect,tkd->ekcd", placing, split_tokens, preferred_element_type=jnp.float32
    )
    outgoing = outgoing.astype(jnp.bfloat16).reshape(devices, capacity, width_dev)
    arrived = lax.all_to_all(outgoing, "dev", split_axis=0, concat_axis=0, tiled=True)
    slot_inputs = arrived.reshape(devices * capacity, width_dev)
    both_weights = jnp.stack(
        [dequantize(gate_values, gate_scales), dequantize(up_values, up_scales)]
    )
    bit_list = list(range(GROUP.bit_length() - 1))
    split_dim = 2
    join_dim = 1
    stacked = jnp.einsum(
        "rd,gdf->grf", slot_inputs, both_weights, preferred_element_type=jnp.float32
    )
    shared = reduce_halves(stacked, split_dim, bit_list)
    hidden_share = (jax.nn.silu(shared[0]) * shared[1]).astype(jnp.bfloat16)
    hidden_whole = join_halves(hidden_share, join_dim, bit_list)
    expert_out = jnp.dot(
        hidden_whole, dequantize(down_values, down_scales), preferred_element_type=jnp.float32
    )
    expert_out = expert_out.astype(jnp.bfloat16).reshape(devices, capacity, width_dev)
    returned = lax.all_to_all(expert_out, "dev", split_axis=0, concat_axis=0, tiled=True)
    returned = returned.reshape(experts, GROUP, capacity, width_dev)
    mixed = jnp.einsum("ect,ekcd->tkd", weighting, returned, preferred_element_type=jnp.float32)
    return mixed.reshape(tok_count, GROUP * width_dev).astype(jnp.bfloat16)


def solution(mesh):
    return jax.shard_map(
        shards,
        mesh=mesh,
        in_specs=(
            P(("rep", "dev"), None),
            P(("rep", "dev"), None),
            P(("rep", "dev"), None),
            P("dev", None),
            P("dev", None),
            P("dev", None),
            P("dev", None),
            P(None, "dev"),
            P(None, "dev"),
        ),
        out_specs=P(("rep", "dev"), None),
        check_vma=False,
    )
```

profile of v0, /device:TPU:0, one launch (start us, length us, event | category | flops | bytes accessed | tf_op | source)
XLA Modules:
  0.0 498.2 jit_solution(1927387002223604220)
XLA Ops:
  0.0 0.8 copy.46
  0.8 0.1 eq.81
  0.9 0.1 eq.77
  1.1 1.2 reduce-window.6
  2.3 0.1 slice.32
  2.4 0.1 copy.48
  2.5 0.1 copy.49
  2.6 0.1 add_bitcast_fusion
  2.7 0.1 reduce_sum.12
  2.9 0.1 copy.50
  2.9 0.7 multiply_add_fusion.1
  3.7 4.7 convolution_convert_fusion.1
  8.4 7.4 %all-to-all-start = ((bf16[32,72,896]{2,1,0:T(8,128)(2,1)}), bf16[32,72,896]{2,1,0:T(8,128)(2,1)}, u32[]{:S(2)}, u32[]{:S(2)}) async-start(bf16[32,72,896]{2,1,0:T(8,128)(2,1)} %bitcast.100), calls=%async_computation | async-start | bytes 8257536 | tf_op jit(solution)/shard_map/all_to_all | solution.py:103
  15.8 0.0 copy-done.4
  15.8 0.3 mul.85
  16.1 2.7 copy.77
  18.8 5.0 %copy.52 = f32[896,1024]{0,1:T(8,128)} copy(f32[896,1024]{1,0:T(8,128)} %bitcast.102) | data formatting | bytes 7340032 | tf_op jit(solution)/shard_map/mul | solution.py:25
  23.9 0.3 mul.88
  24.2 2.7 copy.76
  26.8 5.0 %copy.54 = f32[896,1024]{0,1:T(8,128)} copy(f32[896,1024]{1,0:T(8,128)} %bitcast.103) | data formatting | bytes 7340032 | tf_op jit(solution)/shard_map/mul | solution.py:25
  31.9 3.1 copy.51
  34.9 3.8 copy.53
  38.8 6.2 %fusion.6 = (bf16[1,896,1024]{1,2,0:T(8,128)(2,1)}, bf16[1,896,1024]{1,2,0:T(8,128)(2,1)}) fusion(f32[896,1024]{0,1:T(8,128)} %copy.52, bf16[896,1024]{0,1:T(8,128)(2,1)S(1)} %copy.51, f32[896,1024]{0,1:T(8,128)} %copy.54, bf16[896,1024]{0,1:T(8,128)(2,1)} %copy.53), kind=kLoop, calls=%fused_computation.21 | loop fusion | flops 5505024 | bytes 14680064 | tf_op jit(solution)/shard_map/stack | solution.py:105
  45.0 63.3 %all-to-all-done = bf16[32,72,896]{2,1,0:T(8,128)(2,1)} async-done(((bf16[32,72,896]{2,1,0:T(8,128)(2,1)}), bf16[32,72,896]{2,1,0:T(8,128)(2,1)}, u32[]{:S(2)}, u32[]{:S(2)}) %all-to-all-start) | async-done | bytes 4128800 | tf_op jit(solution)/shard_map/all_to_all | solution.py:103
  108.3 13.6 %fusion.2 = f32[2,1024,2304]{2,1,0:T(8,128)S(1)} fusion(bf16[2304,896,1]{1,0,2:T(8,128)(2,1)} %bitcast.14, bf16[1,896,1024]{1,2,0:T(8,128)(2,1)} %get-tuple-element.10, bf16[1,896,1024]{1,2,0:T(8,128)(2,1)} %get-tuple-element.9), kind=kOutput, calls=%fused_computation.12 | convolution fusion | flops 8457551872 | bytes 26673152 | tf_op jit(solution)/shard_map/rd,gdf->grf/dot_general | solution.py:111
  121.9 4.7 dynamic-slice_bitcast_fusion
  126.6 4.6 copy-done.1
  131.1 0.0 collective-permute-start
  131.1 15.0 %collective-permute-done = f32[2,2304,512]{1,2,0:T(8,128)} collective-permute-done((f32[2,2304,512]{1,2,0:T(8,128)}, f32[2,2304,512]{1,2,0:T(8,128)}, u32[]{:S(2)}, u32[]{:S(2)}) %collective-permute-start) | collective-permute-done | bytes 9437216 | tf_op jit(solution)/shard_map/ppermute | solution.py:17
  146.1 11.2 %bitcast_add_fusion = f32[2,2304,512]{1,2,0:T(8,128)} fusion(f32[2,2304,512]{1,2,0:T(8,128)} %collective-permute-done, f32[2,1024,2304]{2,1,0:T(8,128)} %copy-done.1, s32[]{:T(128)S(6)} %select_n.21), kind=kLoop, calls=%fused_computation | loop fusion | flops 2359296 | bytes 28311556 | tf_op jit(solution)/shard_map/add | solution.py:63
  157.3 5.0 %constant_dynamic-slice_fusion.1 = f32[2,2304,256]{1,2,0:T(8,128)} fusion(f32[2,2304,512]{1,2,0:T(8,128)} %bitcast_add_fusion, s32[]{:T(128)S(6)} %select_n.24), kind=kLoop, calls=%fused_computation.58 | loop fusion | bytes 9437188 | tf_op jit(solution)/shard_map/dynamic_slice | solution.py:60
  162.4 1.3 collective-permute-start.1
  163.7 102.9 %collective-permute-done.1 = f32[2,2304,256]{1,2,0:T(8,128)} collective-permute-done((f32[2,2304,256]{1,2,0:T(8,128)}, f32[2,2304,256]{1,2,0:T(8,128)}, u32[]{:S(2)}, u32[]{:S(2)}) %collective-permute-start.1) | collective-permute-done | bytes 4718624 | tf_op jit(solution)/shard_map/ppermute | solution.py:17
  266.6 4.3 dynamic-slice_add_fusion
  270.9 2.1 copy-done
  273.0 1.6 constant_dynamic-slice_fusion
  274.6 1.3 collective-permute-start.2
  275.9 51.4 %collective-permute-done.2 = f32[2,2304,128]{1,2,0:T(8,128)S(1)} collective-permute-done((f32[2,2304,128]{1,2,0:T(8,128)}, f32[2,2304,128]{1,2,0:T(8,128)S(1)}, u32[]{:S(2)}, u32[]{:S(2)}) %collective-permute-start.2) | collective-permute-done | bytes 2359328 | tf_op jit(solution)/shard_map/ppermute | solution.py:17
  327.3 1.9 dynamic-slice_add_fusion.1
  329.2 0.3 fusion.11
  329.5 1.3 collective-permute-start.3
  330.8 12.4 %collective-permute-done.3 = bf16[2304,128]{0,1:T(8,128)(2,1)S(1)} collective-permute-done((bf16[2304,128]{0,1:T(8,128)(2,1)S(1)}, bf16[2304,128]{0,1:T(8,128)(2,1)S(1)}, u32[]{:S(2)}, u32[]{:S(2)}) %collective-permute-start.3) | collective-permute-done | bytes 589856 | tf_op jit(solution)/shard_map/ppermute | solution.py:17
  343.2 0.1 pad_maximum_fusion.2
  343.3 0.4 constant_dynamic-update-slice_fusion.2
  343.7 0.0 copy-start.3
  343.7 1.4 collective-permute-start.4
  345.1 24.0 %collective-permute-done.4 = bf16[2304,256]{0,1:T(8,128)(2,1)S(1)} collective-permute-done((bf16[2304,256]{0,1:T(8,128)(2,1)S(1)}, bf16[2304,256]{0,1:T(8,128)(2,1)S(1)}, u32[]{:S(2)}, u32[]{:S(2)}) %collective-permute-start.4) | collective-permute-done | bytes 1179680 | tf_op jit(solution)/shard_map/ppermute | solution.py:17
  369.1 0.2 pad_maximum_fusion.1
  369.3 0.1 constant_dynamic-update-slice_fusion.1
  369.4 0.1 collective-permute-start.5
  369.5 0.1 copy.57
  369.6 3.8 copy.56
  373.3 0.8 collective-permute-done.5
  374.1 2.7 pad_maximum_fusion
  376.8 0.0 copy-start.2
  376.8 0.3 constant_dynamic-update-slice_fusion
  377.1 0.3 mul.96
  377.4 0.9 copy-done.2
  378.3 6.9 %convolution_convert_fusion = bf16[2304,896]{1,0:T(8,128)(2,1)} fusion(bf16[2304,1024]{0,1:T(8,128)(2,1)S(1)} %constant_dynamic-update-slice_fusion, f32[112,8,8,128]{3,2,1,0:T(8,128)S(1)} %bitcast.107, bf16[1024,896]{0,1:T(8,128)(2,1)S(1)} %copy-done.2), kind=kOutput, calls=%fused_computation.4 | convolution fusion | flops 4232675328 | bytes 14352384 | tf_op jit(solution)/shard_map/dot_general | solution.py:117
  385.2 4.1 all-to-all-start.1
  389.3 92.5 %all-to-all-done.1 = bf16[32,72,896]{2,1,0:T(8,128)(2,1)} async-done(((bf16[32,72,896]{2,1,0:T(8,128)(2,1)}), bf16[32,72,896]{2,1,0:T(8,128)(2,1)}, u32[]{:S(2)}, u32[]{:S(2)}) %all-to-all-start.1) | async-done | bytes 4128800 | tf_op jit(solution)/shard_map/all_to_all | solution.py:121
  481.8 4.6 copy.75
  486.4 7.1 %dot_general.20 = bf16[7168,72,4]{0,1,2:T(8,128)(2,1)} reshape(bf16[8,896,72,4]{1,0,2,3:T(8,128)(2,1)} %bitcast.101) | data formatting | bytes 8257536 | tf_op jit(solution)/shard_map/ect,ekcd->tkd/dot_general | solution.py:123
  493.6 4.6 fusion
  (15 shorter events, 0.1 us)
Async XLA Ops:
  8.4 7.4 %copy-start.4 = (f32[7,8]{1,0:T(8,128)S(1)}, f32[7,8]{1,0:T(8,128)}, u32[]{:S(2)}) copy-start(f32[7,8]{1,0:T(8,128)} %param.13) | copy-start | bytes 676
  8.4 99.9 %all-to-all-start = ((bf16[32,72,896]{2,1,0:T(8,128)(2,1)}), bf16[32,72,896]{2,1,0:T(8,128)(2,1)}, u32[]{:S(2)}, u32[]{:S(2)}) async-start(bf16[32,72,896]{2,1,0:T(8,128)(2,1)} %bitcast.100), calls=%async_computation | async-start | bytes 8257536 | tf_op jit(solution)/shard_map/all_to_all | solution.py:103
  18.8 5.0 %copy-start.5 = (f32[7,8]{1,0:T(8,128)S(1)}, f32[7,8]{1,0:T(8,128)}, u32[]{:S(2)}) copy-start(f32[7,8]{1,0:T(8,128)} %param.15) | copy-start | bytes 676
  121.8 9.3 %copy-start.1 = (f32[2,1024,2304]{2,1,0:T(8,128)}, f32[2,1024,2304]{2,1,0:T(8,128)S(1)}, u32[]{:S(2)}) copy-start(f32[2,1024,2304]{2,1,0:T(8,128)S(1)} %fusion.2) | copy-start | bytes 56623108
  131.1 15.0 %collective-permute-start = (f32[2,2304,512]{1,2,0:T(8,128)}, f32[2,2304,512]{1,2,0:T(8,128)}, u32[]{:S(2)}, u32[]{:S(2)}) collective-permute-start(f32[2,2304,512]{1,2,0:T(8,128)} %dynamic-slice_bitcast_fusion), channel_id=1, source_target_pairs={{0,1},{1,0},{2,3},{3,2},{4,5},{5,4},{6,7},{7,6},{8,9},{9,8},{10,11... | collective-permute-start | bytes 28311560 | tf_op jit(solution)/shard_map/ppermute | solution.py:17
  162.4 104.2 %collective-permute-start.1 = (f32[2,2304,256]{1,2,0:T(8,128)}, f32[2,2304,256]{1,2,0:T(8,128)}, u32[]{:S(2)}, u32[]{:S(2)}) collective-permute-start(f32[2,2304,256]{1,2,0:T(8,128)} %constant_dynamic-slice_fusion.1), channel_id=1, source_target_pairs={{0,2},{2,0},{1,3},{3,1},{4,6},{6,4},{5,7},{7,5},{8,10},{10,8},{9,1... | collective-permute-start | bytes 14155784 | tf_op jit(solution)/shard_map/ppermute | solution.py:17
  270.9 2.1 copy-start
  274.6 52.7 %collective-permute-start.2 = (f32[2,2304,128]{1,2,0:T(8,128)}, f32[2,2304,128]{1,2,0:T(8,128)S(1)}, u32[]{:S(2)}, u32[]{:S(2)}) collective-permute-start(f32[2,2304,128]{1,2,0:T(8,128)} %constant_dynamic-slice_fusion), channel_id=1, source_target_pairs={{0,4},{4,0},{1,5},{5,1},{2,6},{6,2},{3,7},{7,3},{8,12},{12,8},{9,1... | collective-permute-start | bytes 7077896 | tf_op jit(solution)/shard_map/ppermute | solution.py:17
  329.5 13.7 %collective-permute-start.3 = (bf16[2304,128]{0,1:T(8,128)(2,1)S(1)}, bf16[2304,128]{0,1:T(8,128)(2,1)S(1)}, u32[]{:S(2)}, u32[]{:S(2)}) collective-permute-start(bf16[2304,128]{0,1:T(8,128)(2,1)S(1)} %fusion.11), channel_id=1, source_target_pairs={{0,4},{4,0},{1,5},{5,1},{2,6},{6,2},{3,7},{7,3},{8,12},{12,8},{9,1... | collective-permute-start | bytes 1769480 | tf_op jit(solution)/shard_map/ppermute | solution.py:17
  343.7 25.8 %copy-start.3 = (f32[8,7]{1,0:T(8,128)S(1)}, f32[8,7]{1,0:T(8,128)}, u32[]{:S(2)}) copy-start(f32[8,7]{1,0:T(8,128)} %param.17) | copy-start | bytes 676
  343.7 25.4 %collective-permute-start.4 = (bf16[2304,256]{0,1:T(8,128)(2,1)S(1)}, bf16[2304,256]{0,1:T(8,128)(2,1)S(1)}, u32[]{:S(2)}, u32[]{:S(2)}) collective-permute-start(bf16[2304,256]{0,1:T(8,128)(2,1)S(1)} %constant_dynamic-update-slice_fusion.2), channel_id=1, source_target_pairs={{0,2},{2,0},{1,3},{3,1},{4,6},{6,4},{5,7},{7,5},{8,10},{10,8},{9,1... | collective-permute-start | bytes 3538952 | tf_op jit(solution)/shard_map/ppermute | solution.py:17
  369.4 4.7 collective-permute-start.5
  376.8 1.5 copy-start.2
  385.2 4.1 copy-start.6
  385.2 96.6 %all-to-all-start.1 = ((bf16[32,72,896]{2,1,0:T(8,128)(2,1)}), bf16[32,72,896]{2,1,0:T(8,128)(2,1)}, u32[]{:S(2)}, u32[]{:S(2)}) async-start(bf16[32,72,896]{2,1,0:T(8,128)(2,1)} %bitcast.106), calls=%async_computation.1 | async-start | bytes 8257536 | tf_op jit(solution)/shard_map/all_to_all | solution.py:121
where the time goes:
time: 499 us; the launch traced here: 498 us
  waiting for transfers between devices  362 us (73%)
  local copies, waits for them, and re-layouts  59.7 us (12%)
  matrix products  29.8 us (6%)
  other arithmetic  29.4 us (6%)
  starting transfers between devices  16.8 us (3%)
    ppermute x6, waiting for transfers between devices, from_partner(): return lax.ppermute(block, axis, route)  206 us
    all_to_all x1, waiting for transfers between devices, shards(): lax.all_to_all(expert_out, 'dev', split_axis=0, concat_axis=0, tiled=True)  92.5 us
    all_to_all x1, waiting for transfers between devices, shards(): lax.all_to_all(outgoing, 'dev', split_axis=0, concat_axis=0, tiled=True)  63.3 us
    unnamed x21, local copies, waits for them, and re-layouts  24.5 us
    add x3, other arithmetic, reduce_halves(): stacked = kept_half + from_partner(sent_half, 'dev', bit_number)  17.5 us
    dot_general x1, matrix products, shards(): jnp.einsum('rd,gdf->grf', slot_inputs, both_weights, preferred_element_ty...  13.6 us
    dynamic_slice x3, local copies, waits for them, and re-layouts, reduce_halves(): lax.dynamic_slice_in_dim(stacked, half_size - keep_start, half_size, axis...  11.3 us
    mul x5, local copies, waits for them, and re-layouts, dequantize(): grid * scales[:, None, :, None]  11 us
  transfers between devices with their start and end apart: 8, of which 8 were waited for; matrix products, arithmetic and copies ran while one was open for 7% of the time, Pallas kernels for 0%

commit v1 on v0

v1 whole, which is shorter than its diff:
```python
import functools

import jax
import jax.numpy as jnp
from jax import lax
from jax.experimental import pallas as pl
from jax.experimental.pallas import tpu as pltpu
from jax.sharding import PartitionSpec as P

BLOCK = 128
GROUP = 8
CHIPS = GROUP // 2
MESH = pl.DeviceIdType.MESH


def slot_tables(routes, route_weight, experts, padded, capacity):
    tok_count, top_count = routes.shape
    flat_routes = routes.reshape(-1)
    one_hot = (flat_routes[:, None] == jnp.arange(experts, dtype=jnp.int32)[None, :]).astype(
        jnp.int32
    )
    position = jnp.sum((jnp.cumsum(one_hot, axis=0) - 1) * one_hot, axis=1)
    slot_ids = (flat_routes * padded + position).reshape(tok_count, top_count)
    slot_range = jnp.arange(experts * padded, dtype=jnp.int32)
    placing = jnp.zeros((experts * padded, tok_count), jnp.float32)
    weighting = jnp.zeros((tok_count, experts * padded), jnp.float32)
    for choose in range(top_count):
        match = slot_ids[:, choose][None, :] == slot_range[:, None]
        placing = placing + match.astype(jnp.float32)
        match = slot_ids[:, choose][:, None] == slot_range[None, :]
        weighting = weighting + jnp.where(
            match, route_weight[:, choose].astype(jnp.float32)[:, None], 0.0
        )
    placing = placing.astype(jnp.bfloat16).reshape(experts, padded, tok_count)
    weighting = weighting.astype(jnp.bfloat16).reshape(tok_count, experts, padded)
    none_p, none_w = jnp.zeros_like(placing), jnp.zeros_like(weighting)
    place = jnp.concatenate(
        [
            jnp.concatenate([placing, none_p], axis=2),
            jnp.concatenate([none_p, placing], axis=2),
        ],
        axis=1,
    )
    weigh = jnp.stack(
        [
            jnp.concatenate([weighting, none_w], axis=2).reshape(tok_count, -1),
            jnp.concatenate([none_w, weighting], axis=2).reshape(tok_count, -1),
        ]
    )
    return place, weigh


def kernel(
    experts,
    padded,
    tokens,
    place,
    weigh,
    gate_values,
    gate_scales,
    up_values,
    up_scales,
    down_values,
    down_scales,
    out,
    raw_gate,
    raw_up,
    raw_down,
    both,
    down,
    sent,
    got,
    own,
    part_out,
    part_in,
    hidden,
    back_out,
    back_in,
    raw_sem,
    wide_sem,
    sent_sem,
    got_sem,
    part_out_sem,
    part_in_sem,
    hid_out_sem,
    hid_in_sem,
    back_out_sem,
    back_in_sem,
):
    me = lax.axis_index("dev")
    expert = me // GROUP
    chip = (me % GROUP) // 2
    core = me % 2
    width = gate_values.shape[0]
    cols = part_in.shape[-1]
    half = cols // 2

    def device(group, place_in):
        return group * GROUP + place_in * 2 + core

    def remote(src, dst, send_sem, recv_sem, target):
        return pltpu.make_async_remote_copy(
            src_ref=src,
            dst_ref=dst,
            send_sem=send_sem,
            recv_sem=recv_sem,
            device_id={"dev": target},
            device_id_type=MESH,
        )

    raw = [
        pltpu.make_async_copy(gate_values, raw_gate, raw_sem.at[0]),
        pltpu.make_async_copy(up_values, raw_up, raw_sem.at[1]),
        pltpu.make_async_copy(down_values, raw_down, raw_sem.at[2]),
    ]
    for copy in raw:
        copy.start()

    barrier = pltpu.get_barrier_semaphore()
    partner = expert * GROUP + chip * 2 + (1 - core)
    pl.semaphore_signal(barrier, inc=1, device_id={"dev": partner}, device_id_type=MESH)

    @pl.loop(1, experts * CHIPS)
    def _(step):
        other = lax.rem(expert * CHIPS + chip + step, experts * CHIPS)
        pl.semaphore_signal(
            barrier, inc=1, device_id={"dev": other * 2 + core}, device_id_type=MESH
        )

    pl.semaphore_wait(barrier, experts * CHIPS)

    def dispatch(step, q):
        group = expert ^ step
        return remote(
            sent.at[step, q],
            got.at[expert, chip],
            sent_sem.at[step, q],
            got_sem.at[expert, chip],
            device(group, q),
        )

    def is_self(step, q):
        return jnp.logical_and(step == 0, q == chip)

    @pl.loop(0, experts)
    def _(turn):
        step = experts - 1 - turn
        for q in range(CHIPS):
            low = tokens[:, 2 * q * width : (2 * q + 1) * width]
            high = tokens[:, (2 * q + 1) * width : (2 * q + 2) * width]
            rows = jnp.dot(
                place[expert ^ step],
                jnp.concatenate([low, high], axis=0),
                preferred_element_type=jnp.float32,
            ).astype(jnp.bfloat16)

            @pl.when(is_self(step, q))
            def _():
                got[expert, chip] = rows

            @pl.when(jnp.logical_not(is_self(step, q)))
            def _():
                sent[step, q] = rows
                dispatch(step, q).start()

    for copy in raw:
        copy.wait()

    @pl.loop(0, width // BLOCK)
    def _(r):
        span = pl.ds(pl.multiple_of(r * BLOCK, BLOCK), BLOCK)
        gate = (raw_gate[span, :].astype(jnp.float32) * gate_scales[pl.ds(r, 1), :]).astype(
            jnp.bfloat16
        )
        up = (raw_up[span, :].astype(jnp.float32) * up_scales[pl.ds(r, 1), :]).astype(jnp.bfloat16)
        for q in range(CHIPS):
            both[core, q, span, 0:half] = gate[:, q * half : (q + 1) * half]
            both[core, q, span, half:cols] = up[:, q * half : (q + 1) * half]

    wide = [
        remote(both.at[core], both.at[core], wide_sem.at[0], wide_sem.at[1], partner),
        remote(down.at[core], down.at[core], wide_sem.at[2], wide_sem.at[3], partner),
    ]
    wide[0].start()

    @pl.loop(0, raw_down.shape[0] // BLOCK)
    def _(r):
        span = pl.ds(pl.multiple_of(r * BLOCK, BLOCK), BLOCK)
        down[core, span, :] = (
            raw_down[span, :].astype(jnp.float32) * down_scales[pl.ds(r, 1), :]
        ).astype(jnp.bfloat16)

    wide[1].start()
    for copy in wide:
        copy.wait_recv()

    def part_copy(step, d):
        return remote(
            part_out.at[step, d - 1],
            part_in.at[step, d - 1],
            part_out_sem.at[step, d - 1],
            part_in_sem.at[step, d - 1],
            device(expert, chip ^ d),
        )

    def hidden_copy(step, d):
        return remote(
            hidden.at[step, chip],
            hidden.at[step, chip],
            hid_out_sem.at[step, d - 1],
            hid_in_sem.at[step, d - 1],
            device(expert, chip ^ d),
        )

    def back_copy(step, q):
        return remote(
            back_out.at[step, q],
            back_in.at[chip, expert],
            back_out_sem.at[step, q],
            back_in_sem.at[chip, expert],
            device(expert ^ step, q),
        )

    def widen(step):
        source = expert ^ step
        for q in range(CHIPS):

            @pl.when(jnp.logical_not(is_self(step, q)))
            def _():
                remote(
                    sent.at[step, q],
                    got.at[source, q],
                    sent_sem.at[step, q],
                    got_sem.at[source, q],
                    device(source, q),
                ).wait_recv()

        rows = got[source].astype(jnp.float32)
        low = rows[:, :padded].reshape(CHIPS * padded, width).astype(jnp.bfloat16)
        high = rows[:, padded:].reshape(CHIPS * padded, width).astype(jnp.bfloat16)
        for d in (3, 1, 2, 0):
            total = jnp.dot(low, both[0, chip ^ d], preferred_element_type=jnp.float32)
            total = total + jnp.dot(high, both[1, chip ^ d], preferred_element_type=jnp.float32)
            if d == 0:
                own[step] = total
            else:
                part_out[step, d - 1] = total.astype(jnp.bfloat16)
                part_copy(step, d).start()

    def activate(step):
        total = own[step]
        for d in (1, 2, 3):
            part_copy(step, d).wait_recv()
            total = total + part_in[step, d - 1].astype(jnp.float32)
        gate, up = total[:, :half], total[:, half:]
        hidden[step, chip] = (gate / (1.0 + jnp.exp(-gate)) * up).astype(jnp.bfloat16)
        for d in (3, 1, 2):
            hidden_copy(step, d).start()

    def narrow(step):
        for d in (1, 2, 3):
            remote(
                hidden.at[step, chip],
                hidden.at[step, chip ^ d],
                hid_out_sem.at[step, d - 1],
                hid_in_sem.at[step, d - 1],
                device(expert, chip ^ d),
            ).wait_recv()
        whole = jnp.concatenate([hidden[step, q] for q in range(CHIPS)], axis=1)
        low = jnp.dot(whole, down[0], preferred_element_type=jnp.float32)
        high = jnp.dot(whole, down[1], preferred_element_type=jnp.float32)
        for q in range(CHIPS):
            span = slice(q * padded, (q + 1) * padded)
            rows = jnp.concatenate([low[span], high[span]], axis=0).astype(jnp.bfloat16)

            @pl.when(is_self(step, q))
            def _():
                back_in[chip, expert] = rows

            @pl.when(jnp.logical_not(is_self(step, q)))
            def _():
                back_out[step, q] = rows
                back_copy(step, q).start()

    @pl.loop(0, experts + 1)
    def _(turn):
        @pl.when(turn < experts)
        def _():
            widen(turn)

        @pl.when(turn > 0)
        def _():
            activate(turn - 1)
            narrow(turn - 1)

    for q in range(CHIPS):

        @pl.loop(0, experts)
        def _(step):
            @pl.when(jnp.logical_not(is_self(step, q)))
            def _():
                remote(
                    back_out.at[step, q],
                    back_in.at[q, expert ^ step],
                    back_out_sem.at[step, q],
                    back_in_sem.at[q, expert ^ step],
                    device(expert ^ step, q),
                ).wait_recv()

        rows = back_in[q].reshape(experts * 2 * padded, width)
        for h in range(2):
            start = (2 * q + h) * width
            out[:, start : start + width] = jnp.dot(
                weigh[h], rows, preferred_element_type=jnp.float32
            ).astype(jnp.bfloat16)

    for copy in wide:
        copy.wait_send()

    @pl.loop(0, experts)
    def _(step):
        for d in (1, 2, 3):
            part_copy(step, d).wait_send()
            hidden_copy(step, d).wait_send()
        for q in range(CHIPS):

            @pl.when(jnp.logical_not(is_self(step, q)))
            def _():
                dispatch(step, q).wait_send()
                back_copy(step, q).wait_send()


def shards(
    tokens,
    routes,
    route_weight,
    gate_values,
    gate_scales,
    up_values,
    up_scales,
    down_values,
    down_scales,
):
    devices = lax.axis_size("dev")
    experts = devices // GROUP
    tok_count, model = tokens.shape
    top_count = routes.shape[1]
    capacity = min(tok_count, tok_count * top_count * 9 // (8 * experts))
    padded = -(-capacity // 8) * 8
    width, units = gate_values.shape
    cols = 2 * units // CHIPS
    place, weigh = slot_tables(routes, route_weight, experts, padded, capacity)
    spread = functools.partial(jnp.repeat, repeats=BLOCK, axis=1)
    vmem = pl.BlockSpec(memory_space=pltpu.VMEM)
    anywhere = pl.BlockSpec(memory_space=pl.ANY)
    bf16 = jnp.bfloat16
    rows = CHIPS * padded
    dma = pltpu.SemaphoreType.DMA
    return pl.pallas_call(
        functools.partial(kernel, experts, padded),
        out_shape=jax.ShapeDtypeStruct((tok_count, model), bf16),
        in_specs=[vmem, vmem, vmem, anywhere, vmem, anywhere, vmem, anywhere, vmem],
        out_specs=vmem,
        scratch_shapes=[
            pltpu.VMEM((width, units), bf16),
            pltpu.VMEM((width, units), bf16),
            pltpu.VMEM((units, width), bf16),
            pltpu.VMEM((2, CHIPS, width, cols), bf16),
            pltpu.VMEM((2, units, width), bf16),
            pltpu.VMEM((experts, CHIPS, 2 * padded, width), bf16),
            pltpu.VMEM((experts, CHIPS, 2 * padded, width), bf16),
            pltpu.VMEM((experts, rows, cols), jnp.float32),
            pltpu.VMEM((experts, CHIPS - 1, rows, cols), bf16),
            pltpu.VMEM((experts, CHIPS - 1, rows, cols), bf16),
            pltpu.VMEM((experts, CHIPS, rows, cols // 2), bf16),
            pltpu.VMEM((experts, CHIPS, 2 * padded, width), bf16),
            pltpu.VMEM((CHIPS, experts, 2 * padded, width), bf16),
            dma((3,)),
            dma((4,)),
            dma((experts, CHIPS)),
            dma((experts, CHIPS)),
            dma((experts, CHIPS - 1)),
            dma((experts, CHIPS - 1)),
            dma((experts, CHIPS - 1)),
            dma((experts, CHIPS - 1)),
            dma((experts, CHIPS)),
            dma((CHIPS, experts)),
        ],
        compiler_params=pltpu.CompilerParams(
            collective_id=0, has_side_effects=True, vmem_limit_bytes=60 * 1024 * 1024
        ),
    )(
        tokens,
        place,
        weigh,
        gate_values,
        spread(gate_scales),
        up_values,
        spread(up_scales),
        down_values,
        spread(down_scales),
    )


def solution(mesh):
    return jax.shard_map(
        shards,
        mesh=mesh,
        in_specs=(
            P(("rep", "dev"), None),
            P(("rep", "dev"), None),
            P(("rep", "dev"), None),
            P("dev", None),
            P("dev", None),
            P("dev", None),
            P("dev", None),
            P(None, "dev"),
            P(None, "dev"),
        ),
        out_specs=P(("rep", "dev"), None),
        check_vma=False,
    )
```

time: 499 us -> 287 us (0.58)
  the two profiles are of different devices: /device:TPU:0 before, /device:TPU:23 now
where the time goes in v1:
time: 287 us
  Pallas kernels  275 us (96%)
  local copies, waits for them, and re-layouts  7.68 us (3%)
  other arithmetic  4.54 us (2%)
    pallas_call x1, Pallas kernels, shards(): pl.pallas_call(functools.partial(kernel, experts, padded), out_shape=jax....  275 us

profile of v1, /device:TPU:23, one launch (start us, length us, event | category | flops | bytes accessed | tf_op | source)
XLA Modules:
  0.0 287.0 jit_solution(13726285662121281323)
XLA Ops:
  0.0 0.0 copy-start
  0.0 0.7 bitcast_convert_fusion.1
  0.7 0.8 copy.38
  1.5 0.7 broadcast_bitcast_fusion.down_scales
  2.2 0.0 copy-done
  2.2 0.1 broadcast_bitcast_fusion.2
  2.3 0.8 broadcast_bitcast_fusion.1
  3.0 0.6 copy_bitcast_fusion
  3.7 0.8 copy.31
  4.4 0.1 eq.107
  4.6 0.1 eq.103
  4.7 1.2 reduce-window.6
  6.0 0.1 slice.26
  6.0 0.1 copy.33
  6.2 0.1 copy.34
  6.3 0.1 add_bitcast_fusion
  6.4 0.1 reduce_sum.12
  6.5 0.1 copy.35
  6.6 0.7 multiply_add_fusion.1
  7.3 0.1 add_convert_fusion
  7.4 0.1 add_convert_fusion.1
  7.5 0.7 fusion.2.place
  8.3 0.2 copy.37
  8.5 0.2 copy.36
  8.6 0.8 pad_maximum_fusion.weigh
  9.4 274.8 %shard_map.91 = bf16[128,7168]{1,0:T(8,128)(2,1)} custom-call(bf16[128,7168]{1,0:T(8,128)(2,1)} %tokens.1, bf16[4,144,256]{2,1,0:T(8,128)(2,1)} %fusion.2.place, bf16[2,128,576]{2,1,0:T(8,128)(2,1)} %pad_maximum_fusion.weigh, bf16[896,1024]{1,0:T(8,128)(2,1)} %gate_values.1, f32[7,1024]{1,0:T(8,128)} %get-tuple-element.12.gate_scales, ...), custom_call_target="tpu_custom_call" | custom-call | tf_op jit(solution)/shard_map/pallas_call | solution.py:359
  284.2 2.8 copy.46
  (7 shorter events, 0.1 us)
Async XLA Ops:
  0.0 2.2 copy-start

commit v2 on v1

--- a/solution.py
+++ b/solution.py
@@ -144,7 +144,7 @@
 
     @pl.loop(0, experts)
     def _(turn):
-        step = experts - 1 - turn
+        step = turn ^ (experts - 1)
         for q in range(CHIPS):
             low = tokens[:, 2 * q * width : (2 * q + 1) * width]
             high = tokens[:, (2 * q + 1) * width : (2 * q + 2) * width]
@@ -161,7 +161,12 @@
             @pl.when(jnp.logical_not(is_self(step, q)))
             def _():
                 sent[step, q] = rows
-                dispatch(step, q).start()
+
+        for d in (3, 1, 2, 0):
+
+            @pl.when(jnp.logical_not(is_self(step, chip ^ d)))
+            def _():
+                dispatch(step, chip ^ d).start()
 
     for copy in raw:
         copy.wait()
@@ -280,18 +285,23 @@
             @pl.when(jnp.logical_not(is_self(step, q)))
             def _():
                 back_out[step, q] = rows
-                back_copy(step, q).start()
+
+        for d in (3, 1, 2, 0):
+
+            @pl.when(jnp.logical_not(is_self(step, chip ^ d)))
+            def _():
+                back_copy(step, chip ^ d).start()
 
     @pl.loop(0, experts + 1)
     def _(turn):
         @pl.when(turn < experts)
         def _():
-            widen(turn)
+            widen(turn ^ (experts - 1))
 
         @pl.when(turn > 0)
         def _():
-            activate(turn - 1)
-            narrow(turn - 1)
+            activate((turn - 1) ^ (experts - 1))
+            narrow((turn - 1) ^ (experts - 1))
 
     for q in range(CHIPS):
 

time: 287 us -> 253 us (0.88)
  the two profiles are of different devices: /device:TPU:23 before, /device:TPU:0 now
where the time goes in v2:
time: 253 us; the launch traced here: 252 us
  Pallas kernels  239 us (94%)
  local copies, waits for them, and re-layouts  7.68 us (3%)
  other arithmetic  4.54 us (2%)
    pallas_call x1, Pallas kernels, shards(): pl.pallas_call(functools.partial(kernel, experts, padded), out_shape=jax....  239 us
    unnamed x7, local copies, waits for them, and re-layouts  5.23 us

profile of v2, /device:TPU:0, one launch (start us, length us, event | category | flops | bytes accessed | tf_op | source)
XLA Modules:
  0.0 251.5 jit_solution(3728043044257876255)
XLA Ops:
  0.0 0.0 copy-start
  0.0 0.7 bitcast_convert_fusion.1
  0.7 0.8 copy.38
  1.5 0.7 broadcast_bitcast_fusion.down_scales
  2.2 0.0 copy-done
  2.2 0.1 broadcast_bitcast_fusion.2
  2.3 0.8 broadcast_bitcast_fusion.1
  3.0 0.6 copy_bitcast_fusion
  3.7 0.8 copy.31
  4.4 0.1 eq.107
  4.6 0.1 eq.103
  4.7 1.2 reduce-window.6
  6.0 0.1 slice.26
  6.0 0.1 copy.33
  6.2 0.1 copy.34
  6.3 0.1 add_bitcast_fusion
  6.4 0.1 reduce_sum.12
  6.5 0.1 copy.35
  6.6 0.7 multiply_add_fusion.1
  7.3 0.1 add_convert_fusion
  7.4 0.1 add_convert_fusion.1
  7.5 0.7 fusion.2.place
  8.3 0.2 copy.37
  8.5 0.2 copy.36
  8.6 0.8 pad_maximum_fusion.weigh
  9.4 239.2 %shard_map.91 = bf16[128,7168]{1,0:T(8,128)(2,1)} custom-call(bf16[128,7168]{1,0:T(8,128)(2,1)} %tokens.1, bf16[4,144,256]{2,1,0:T(8,128)(2,1)} %fusion.2.place, bf16[2,128,576]{2,1,0:T(8,128)(2,1)} %pad_maximum_fusion.weigh, bf16[896,1024]{1,0:T(8,128)(2,1)} %gate_values.1, f32[7,1024]{1,0:T(8,128)} %get-tuple-element.12.gate_scales, ...), custom_call_target="tpu_custom_call" | custom-call | tf_op jit(solution)/shard_map/pallas_call | solution.py:369
  248.7 2.8 %copy.46 = bf16[128,7168]{1,0:T(8,128)(2,1)} copy(bf16[128,7168]{1,0:T(8,128)(2,1)} %shard_map.91) | data formatting | bytes 3670016
  (7 shorter events, 0.1 us)
Async XLA Ops:
  0.0 2.2 copy-start
